TPU v7x, 1024 devices: a whole 4x4x32 slice. The times are simulated.
1024 devices in a mesh: replica: 16 (over z_lo), shard: 64 (over z_hi, y, x, core).
Axes of the slice: x: 4, y: 4, z: 32 (z_hi: 2, z_lo: 16; z = z_hi * 16 + z_lo), core: 2. Of those that a mesh axis runs over, the one named last changes fastest.
Arguments:
- pooled_grad: float32 [131072, 128], P(('replica', 'shard')), may hold values from -1.5 to 1.5
- bag_lengths: int32 [1024, 128], P(('replica', 'shard')), may hold values from 1 to 16, 1024 in all within a row
- slot_ids: int32 [1048576], P(('replica', 'shard')), may hold values from 0 to 511, as said below
- offsets: int32 [1048576], P(('replica', 'shard')), may hold values from 0 to 127
- touched_blocks: int32 [512], P('shard'), may hold values from 0 to 23, as said below
- embedding_table: float32 [196608, 128], P('shard'), may hold values from -3 to 3
- accumulator: float32 [196608], P('shard'), may hold values from 0.1 to 2
Outputs:
- new_table: float32 [196608, 128], P('shard')
- new_accumulator: float32 [196608], P('shard')
Inputs may be any that keep to these rules, and one draw needn't show every extreme that they name: `slot_ids`: of the 1024 lookups of one device, exactly 32 name slots of one index o of shard (slots o * 8 to (o + 1) * 8 - 1), and every other index is named by at most 32 of them. `touched_blocks`: the 8 entries of one index of shard are distinct.
All inputs are finite; a program needn't handle non-finite values.
Results may differ from a plain program's by a relative error of at most 0.0003.
Values sent between devices are 32-bit elements; how exact they have to be, the bound alone decides.
A program may use at most 32 MiB of HBM per device.

v0:
```python
import jax
import jax.numpy as jnp
from jax import lax
from jax.sharding import PartitionSpec as P

ROW_BLOCK = 128


learning_rate = 0.5
epsilon = 1e-08


def accumulate(values, row_ids, block_count):
    block_rows = jnp.arange(ROW_BLOCK, dtype=jnp.int32)

    def one_block(block):
        one_hot = (row_ids[None, :] == block * ROW_BLOCK + block_rows[:, None]).astype(jnp.float32)
        return jnp.dot(
            one_hot, values, preferred_element_type=jnp.float32, precision=lax.Precision.HIGHEST
        )

    summed = lax.map(one_block, jnp.arange(block_count, dtype=jnp.int32))
    return summed.reshape(block_count * ROW_BLOCK, values.shape[1])


def adagrad(table_rows, accum_rows, gradient):
    new_acc = accum_rows + jnp.mean(gradient * gradient, axis=1)
    new_rows = table_rows - learning_rate * gradient / (jnp.sqrt(new_acc) + epsilon)[:, None]
    return (new_acc, new_rows)


def on_device(
    pooled_grad, bag_lengths, slot_ids, offsets, touched_blocks, embedding_table, accumulator
):
    groups = lax.axis_size("shard")
    lookups = slot_ids.shape[0]
    capacity = 2 * lookups // groups
    blocks_held = touched_blocks.shape[0]
    width = pooled_grad.shape[1]
    samples = pooled_grad.shape[0]
    lengths = bag_lengths[0]
    sample_index = jnp.arange(samples, dtype=jnp.int32)
    lower = (sample_index[:, None] >= sample_index[None, :]).astype(jnp.int32)
    bag_ends = jnp.sum(lower * lengths[None, :], axis=1)
    positions = jnp.arange(lookups, dtype=jnp.int32)
    sample = jnp.sum((bag_ends[None, :] <= positions[:, None]).astype(jnp.int32), axis=1)
    owner_index = slot_ids // blocks_held
    local_id = (slot_ids - owner_index * blocks_held) * ROW_BLOCK + offsets
    earlier = (owner_index[:, None] == owner_index[None, :]) & (
        positions[None, :] < positions[:, None]
    )
    slot_rank = jnp.sum(earlier.astype(jnp.int32), axis=1)
    send_slot = owner_index * capacity + slot_rank
    placed = send_slot[None, :] == jnp.arange(groups * capacity, dtype=jnp.int32)[:, None]
    sample_hot = (sample[:, None] == sample_index[None, :]).astype(jnp.bfloat16)
    picker = jnp.dot(placed.astype(jnp.bfloat16), sample_hot, preferred_element_type=jnp.float32)
    outgoing = jnp.dot(
        picker, pooled_grad, preferred_element_type=jnp.float32, precision=lax.Precision.HIGHEST
    )
    outgoing = outgoing.reshape(groups, capacity, width)
    out_ids = jnp.sum(jnp.where(placed, local_id[None, :] + 1, 0), axis=1) - 1
    out_ids = out_ids.reshape(groups, capacity)
    incoming, in_ids = (
        lax.all_to_all(outgoing, "shard", split_axis=0, concat_axis=0, tiled=True),
        lax.all_to_all(out_ids, "shard", split_axis=0, concat_axis=0, tiled=True),
    )
    incoming = incoming.reshape(groups * capacity, width)
    in_ids = in_ids.reshape(groups * capacity)
    block_count = embedding_table.shape[0] // ROW_BLOCK
    block_slot = in_ids // ROW_BLOCK
    within = in_ids % ROW_BLOCK
    matches = (block_slot[:, None] == jnp.arange(blocks_held, dtype=jnp.int32)[None, :]).astype(
        jnp.int32
    )
    held_block = jnp.sum(matches * touched_blocks[None, :], axis=1)
    row_ids = jnp.where(in_ids >= 0, held_block * ROW_BLOCK + within, -1)
    gradient = accumulate(incoming, row_ids, block_count)
    summed = lax.psum(gradient, "replica")
    new_accumulator, new_table = adagrad(embedding_table, accumulator, summed)
    return (new_table, new_accumulator)


def solution(mesh):
    return jax.shard_map(
        on_device,
        mesh=mesh,
        in_specs=(
            P(("replica", "shard"), None),
            P(("replica", "shard"), None),
            P(("replica", "shard")),
            P(("replica", "shard")),
            P("shard"),
            P("shard", None),
            P("shard"),
        ),
        out_specs=(P("shard", None), P("shard")),
        check_vma=False,
    )
```

profile of v0, /device:TPU:2, one launch (start us, length us, event | category | flops | bytes accessed | tf_op | source)
XLA Modules:
  0.0 628.7 jit_solution(7195852592322587092)
XLA Ops:
  10.8 34.5 %all-to-all-start = ((s32[64,1,32]{2,1,0:T(1,128)}), s32[64,1,32]{2,1,0:T(1,128)S(1)}, u32[]{:S(2)}, u32[]{:S(2)}) async-start(s32[64,1,32]{2,1,0:T(1,128)} %bitcast), calls=%async_computation | async-start | bytes 65536 | tf_op jit(solution)/shard_map/all_to_all | solution.py:65
  46.3 1.6 fusion.6
  47.9 2.0 fusion.16
  49.9 20.7 %all-to-all-done = s32[64,1,32]{2,1,0:T(1,128)S(1)} async-done(((s32[64,1,32]{2,1,0:T(1,128)}), s32[64,1,32]{2,1,0:T(1,128)S(1)}, u32[]{:S(2)}, u32[]{:S(2)}) %all-to-all-start) | async-done | bytes 8224 | tf_op jit(solution)/shard_map/all_to_all | solution.py:65
  70.6 6.7 %all-to-all-start.1 = ((f32[64,32,128]{2,1,0:T(8,128)}), f32[64,32,128]{2,1,0:T(8,128)S(1)}, u32[]{:S(2)}, u32[]{:S(2)}) async-start(f32[64,32,128]{2,1,0:T(8,128)} %bitcast.2), calls=%async_computation.1 | async-start | bytes 2097152 | tf_op jit(solution)/shard_map/all_to_all | solution.py:64
  78.9 45.5 %all-to-all-done.1 = f32[64,32,128]{2,1,0:T(8,128)S(1)} async-done(((f32[64,32,128]{2,1,0:T(8,128)}), f32[64,32,128]{2,1,0:T(8,128)S(1)}, u32[]{:S(2)}, u32[]{:S(2)}) %all-to-all-start.1) | async-done | bytes 1048608 | tf_op jit(solution)/shard_map/all_to_all | solution.py:64
  124.4 66.5 %while.11 = (s32[]{:T(128)}, f32[24,128,128]{2,1,0:T(8,128)}, s32[2048]{0:T(1024)S(1)}, s32[24]{0:T(128)S(1)}, f32[2048,128]{1,0:T(8,128)S(1)}, /*index=5*/s32[]{:T(128)}, s32[1]{0:T(128)}) while((s32[]{:T(128)}, f32[24,128,128]{2,1,0:T(8,128)}, s32[2048]{0:T(1024)S(1)}, s32[24]{0:T(128)S(1)}, f32[2048,128]{1,0:T(8,128)S(1)}, ...), condition=%wide.region_6.7_spmd.clone, body=%wide.region_5.6_spmd.clone.sunk | while | flops 402915456 | bytes 1123445 | solution.py:22
  125.7 1.4 fusion.25
  131.3 1.4 fusion.25
  134.1 1.4 fusion.25
  139.6 1.4 fusion.25
  142.4 1.4 fusion.25
  147.9 1.4 fusion.25
  150.7 1.4 fusion.25
  156.2 1.4 fusion.25
  159.0 1.4 fusion.25
  164.5 1.4 fusion.25
  167.3 1.4 fusion.25
  175.6 1.4 fusion.25
  178.4 1.4 fusion.25
  183.9 1.4 fusion.25
  190.9 426.6 %all-reduce.2.cloned.1.call-done = f32[3072,128]{1,0:T(8,128)} async-done(((f32[3072,128]{1,0:T(8,128)}), f32[3072,128]{1,0:T(8,128)}) %all-reduce.2.cloned.1.call-update) | async-done | bytes 1572880 | tf_op jit(solution)/shard_map/psum | solution.py:78
  617.5 2.0 multiply_reduce_fusion
  620.2 1.7 divide_subtract_fusion
  (87 shorter events, 36.8 us)
Async XLA Ops:
  7.2 40.8 %copy-start = (f32[128,128]{1,0:T(8,128)S(1)}, f32[128,128]{1,0:T(8,128)}, u32[]{:S(2)}) copy-start(f32[128,128]{1,0:T(8,128)} %param.9) | copy-start | bytes 196612
  10.8 59.8 %all-to-all-start = ((s32[64,1,32]{2,1,0:T(1,128)}), s32[64,1,32]{2,1,0:T(1,128)S(1)}, u32[]{:S(2)}, u32[]{:S(2)}) async-start(s32[64,1,32]{2,1,0:T(1,128)} %bitcast), calls=%async_computation | async-start | bytes 65536 | tf_op jit(solution)/shard_map/all_to_all | solution.py:65
  49.9 28.9 %copy-start.4 = (s32[8]{0:T(128)S(1)}, s32[8]{0:T(128)}, u32[]{:S(2)}) copy-start(s32[8]{0:T(128)} %param.13) | copy-start | bytes 100
  70.6 53.8 %all-to-all-start.1 = ((f32[64,32,128]{2,1,0:T(8,128)}), f32[64,32,128]{2,1,0:T(8,128)S(1)}, u32[]{:S(2)}, u32[]{:S(2)}) async-start(f32[64,32,128]{2,1,0:T(8,128)} %bitcast.2), calls=%async_computation.1 | async-start | bytes 2097152 | tf_op jit(solution)/shard_map/all_to_all | solution.py:64
  77.3 540.3 %all-reduce.2.cloned.1.call-start = ((), (), s32[]{:S(2)}) async-start(), calls=%async_computation.2 | async-start | bytes 3145728 | tf_op jit(solution)/shard_map/psum | solution.py:78
  190.9 428.7 %copy-start.3 = (f32[3072]{0:T(1024)S(1)}, f32[3072]{0:T(1024)}, u32[]{:S(2)}) copy-start(f32[3072]{0:T(1024)} %param.15) | copy-start | bytes 36868
  190.9 429.3 %copy-start.2 = (f32[3072,128]{1,0:T(8,128)S(1)}, f32[3072,128]{1,0:T(8,128)}, u32[]{:S(2)}) copy-start(f32[3072,128]{1,0:T(8,128)} %param.14) | copy-start | bytes 4718596
  617.5 2.6 copy-start.1
Sparse Core Ops, SparseCore 0:
  191.0 426.4 all-reduce.1
where the time goes:
time: 629 us
  waiting for transfers between devices  493 us (78%)
  starting transfers between devices  41.2 us (7%)
  matrix products  37.2 us (6%)
  local copies, waits for them, and re-layouts  17.3 us (3%)
  loops' own time  16.9 us (3%)
  between operations  14.1 us (2%)
  other arithmetic  9.16 us (1%)
    psum x1, waiting for transfers between devices, on_device(): summed = lax.psum(gradient, 'replica')  427 us
    all_to_all x1, waiting for transfers between devices, on_device(): lax.all_to_all(outgoing, 'shard', split_axis=0, concat_axis=0, tiled=True)  45.5 us
    all_to_all x1, starting transfers between devices, on_device(): lax.all_to_all(out_ids, 'shard', split_axis=0, concat_axis=0, tiled=True)  34.5 us
    dot_general x24, matrix products, one_block(): jnp.dot(one_hot, values, preferred_element_type=jnp.float32, precision=la...  33.6 us
    all_to_all x1, waiting for transfers between devices, on_device(): lax.all_to_all(out_ids, 'shard', split_axis=0, concat_axis=0, tiled=True)  20.7 us
    another operation x1, loops' own time, accumulate(): summed = lax.map(one_block, jnp.arange(block_count, dtype=jnp.int32))  16.9 us
    dynamic_slice x24, local copies, waits for them, and re-layouts, accumulate(): summed = lax.map(one_block, jnp.arange(block_count, dtype=jnp.int32))  15.9 us
  transfers between devices with their start and end apart: 3, of which 3 were waited for; matrix products, arithmetic and copies ran while one was open for 1% of the time, Pallas kernels for 0%

commit v1 on v0

v1 whole, which is shorter than its diff:
```python
import jax
import jax.numpy as jnp
from jax import lax
from jax.experimental import pallas as pl
from jax.experimental.pallas import tpu as pltpu
from jax.sharding import PartitionSpec as P

MESH = pl.DeviceIdType.MESH
F32, BF16, I32 = jnp.float32, jnp.bfloat16, jnp.int32

learning_rate = 0.5
epsilon = 1e-08

GROUP = 64
CAP = 32
BLOCKS = 8
ROWS = 128
D = 128
LOOKUPS = 1024


def dot(a, b):
    return lax.dot_general(a, b, (((1,), (0,)), ((), ())), preferred_element_type=F32)


def dot_t(a, b):
    return lax.dot_general(a, b, (((1,), (1,)), ((), ())), preferred_element_type=F32)


def iota(shape, dim):
    return lax.broadcasted_iota(I32, shape, dim)


def halves(x):
    high = x.astype(BF16)
    return high, (x - high.astype(F32)).astype(BF16)


def rows_side_by_side(parts):
    return jnp.concatenate(parts, axis=1)


def gather_kernel(
    grad_ref, len_ref, slot_ref, off_ref, total_ref,
    sbuf, rbuf, sid, rid, rhl, looked, partial, left_in, right_in,
    send_sem, recv_sem, sid_sem, rid_sem, red_send, left_sem, right_sem, out_send, out_sem,
):
    replica, shard = lax.axis_index("replica"), lax.axis_index("shard")
    z = lax.div(shard, 32) * 16 + replica
    within = lax.rem(shard, 32)
    parity = lax.rem(z, 2)
    me = parity * 32 + within

    def device(z_at, place):
        return (lax.rem(z_at, 16), lax.div(z_at, 16) * 32 + place)

    def member(o):
        return device(z - parity + lax.div(o, 32), lax.rem(o, 32))

    left = device(lax.rem(z + 30, 32), within)
    right = device(lax.rem(z + 2, 32), within)
    twin = device(z + 1 - 2 * parity, within)

    barrier = pltpu.get_barrier_semaphore()

    def greet(i, carry):
        pl.semaphore_signal(
            barrier, inc=1, device_id=member(lax.rem(me + i, GROUP)), device_id_type=MESH
        )
        return carry

    lax.fori_loop(1, GROUP, greet, 0)
    for other in (left, right):
        pl.semaphore_signal(barrier, inc=1, device_id=other, device_id_type=MESH)

    row, col = iota((128, 128), 0), iota((128, 128), 1)
    upto = (row <= col).astype(F32).astype(BF16)
    before = (row < col).astype(F32).astype(BF16)
    lengths = len_ref[...].astype(F32)
    ends = dot(jnp.broadcast_to(lengths, (8, 128)).astype(BF16), upto)[0:1, :]
    starts = ends - lengths
    position = iota((LOOKUPS, 128), 0).astype(F32)
    sample_hot = jnp.where((position >= starts) & (position < ends), 1.0, 0.0).astype(BF16)
    high, low = halves(grad_ref[...])
    looked[...] = dot(sample_hot, jnp.concatenate([high, low], axis=1)).astype(BF16)

    slots = slot_ref[...]
    owner = lax.shift_right_logical(slots, 3)
    listed = slots - owner * BLOCKS
    owner_hot = [
        jnp.where(owner[b : b + 1, :] == iota((GROUP, 128), 0), 1.0, 0.0) for b in range(8)
    ]
    counts = dot(jnp.concatenate(owner_hot, axis=0).astype(BF16), before)
    seen = jnp.zeros((GROUP, 1), F32)
    ranks = []
    for b in range(8):
        earlier = counts[b * GROUP : (b + 1) * GROUP, :] + seen
        ranks.append(jnp.sum(owner_hot[b] * earlier, axis=0, keepdims=True))
        seen = seen + jnp.sum(owner_hot[b], axis=1, keepdims=True)
    rank = rows_side_by_side(ranks)
    owner_row = rows_side_by_side([owner[b : b + 1, :] for b in range(8)])
    place = owner_row * CAP + rank.astype(I32)
    owners = rows_side_by_side([h.astype(BF16) for h in owner_hot])
    lane = rank.astype(I32) + CAP * lax.rem(me, 4)
    at_lane = lane == iota((128, LOOKUPS), 0)
    listed_row = rows_side_by_side([listed[b : b + 1, :] for b in range(8)]).astype(F32)
    offset_row = rows_side_by_side([off_ref[b : b + 1, :] for b in range(8)]).astype(F32)
    ids = 128.0 * dot_t(owners, jnp.where(at_lane, listed_row + 1.0, 0.0).astype(BF16)) + dot_t(
        owners, jnp.where(at_lane, offset_row, 0.0).astype(BF16)
    )
    for o in range(GROUP):
        sid[o] = ids[o : o + 1, :]

    pl.semaphore_wait(barrier, GROUP + 1)

    def value_copy(o, src):
        return pltpu.make_async_remote_copy(
            sbuf.at[o], rbuf.at[src], send_sem.at[o], recv_sem.at[src],
            device_id=member(o), device_id_type=MESH,
        )

    def id_copy(o, src):
        return pltpu.make_async_remote_copy(
            sid.at[o], rid.at[src], sid_sem.at[o], rid_sem.at[src],
            device_id=member(o), device_id_type=MESH,
        )

    my_quad = lax.div(me, 4)

    def send(i, carry):
        quad = lax.rem(my_quad + 1 + i, 16)
        hot = jnp.where(place - quad * 128 == iota((128, LOOKUPS), 0), 1.0, 0.0).astype(BF16)
        both = dot(hot, looked[...])
        sbuf[pl.ds(quad * 4, 4)] = (both[:, :D] + both[:, D:]).reshape(4, CAP, D)
        for r in range(4):
            o = quad * 4 + r

            @pl.when(o != me)
            def _():
                value_copy(o, me).start()
                id_copy(o, me).start()

        return carry

    lax.fori_loop(0, 16, send, 0)
    rbuf[me] = sbuf[me]
    rid[me] = sid[me]

    def arrive(i, carry):
        src = lax.rem(me + i, GROUP)
        value_copy(src, src).wait_recv()
        id_copy(src, src).wait_recv()
        return carry

    lax.fori_loop(1, GROUP, arrive, 0)

    id_row = rows_side_by_side(
        [rid[4 * g] + rid[4 * g + 1] + rid[4 * g + 2] + rid[4 * g + 3] for g in range(16)]
    ).astype(I32)
    high, low = halves(rbuf[...].reshape(GROUP * CAP, D))
    rhl[:, :D] = high
    rhl[:, D:] = low

    def own_block(j):
        hot = jnp.where(
            id_row - (j + 1) * ROWS == iota((ROWS, GROUP * CAP), 0), 1.0, 0.0
        ).astype(BF16)
        both = dot(hot, rhl[...])
        return both[:, :D] + both[:, D:]

    seat = lax.rem(lax.div(z, 2) - 8 * parity + 16, 16)

    def left_copy(j):
        return pltpu.make_async_remote_copy(
            partial.at[j], left_in.at[j], red_send.at[j], left_sem.at[j],
            device_id=left, device_id_type=MESH,
        )

    def right_copy(j):
        return pltpu.make_async_remote_copy(
            partial.at[j], right_in.at[j], red_send.at[j], right_sem.at[j],
            device_id=right, device_id_type=MESH,
        )

    def reduce_step(t, carry):
        jl = lax.rem(seat + 8 + t, 16)
        jr = lax.rem(seat + 23 - t, 16)

        @pl.when(jl < BLOCKS)
        def _():
            partial[jl] = own_block(jl)

        @pl.when((jr < BLOCKS) & (t < 7))
        def _():
            partial[jr] = own_block(jr)

        @pl.when(jl < BLOCKS)
        def _():
            @pl.when(t > 0)
            def _():
                left_copy(jl).wait_recv()
                partial[jl] = partial[jl] + left_in[jl]

            left_copy(jl).start()

        @pl.when((jr < BLOCKS) & (t < 7))
        def _():
            @pl.when(t > 0)
            def _():
                right_copy(jr).wait_recv()
                partial[jr] = partial[jr] + right_in[jr]

            right_copy(jr).start()

        return carry

    lax.fori_loop(0, 8, reduce_step, 0)

    def out_copy(j, way, target):
        return pltpu.make_async_remote_copy(
            total_ref.at[j], total_ref.at[j], out_send.at[j, way], out_sem.at[j],
            device_id=target, device_id_type=MESH,
        )

    holds = seat < BLOCKS

    @pl.when(holds)
    def _():
        mine = own_block(seat)
        left_copy(seat).wait_recv()
        right_copy(seat).wait_recv()
        total_ref[seat] = mine + left_in[seat] + right_in[seat]

        @pl.when(seat > 0)
        def _():
            out_copy(seat, 0, left).start()

        @pl.when(seat < 7)
        def _():
            out_copy(seat, 1, right).start()

        out_copy(seat, 2, twin).start()

        def pass_on(s, carry):
            @pl.when(seat + s < BLOCKS)
            def _():
                out_copy(seat + s, 0, left).wait_recv()

                @pl.when(seat > 0)
                def _():
                    out_copy(seat + s, 0, left).start()

                out_copy(seat + s, 2, twin).start()

            @pl.when(seat - s >= 0)
            def _():
                out_copy(seat - s, 1, right).wait_recv()

                @pl.when(seat < 7)
                def _():
                    out_copy(seat - s, 1, right).start()

                out_copy(seat - s, 2, twin).start()

            return carry

        lax.fori_loop(1, 8, pass_on, 0)

        def sent(j, carry):
            @pl.when((j >= seat) & (seat > 0))
            def _():
                out_copy(j, 0, left).wait_send()

            @pl.when((j <= seat) & (seat < 7))
            def _():
                out_copy(j, 1, right).wait_send()

            out_copy(j, 2, twin).wait_send()
            return carry

        lax.fori_loop(0, BLOCKS, sent, 0)

    @pl.when(jnp.logical_not(holds))
    def _():
        def land(j, carry):
            out_copy(j, 2, twin).wait_recv()
            return carry

        lax.fori_loop(0, BLOCKS, land, 0)

    def reduced(j, carry):
        @pl.when(j != seat)
        def _():
            left_copy(j).wait_send()

        return carry

    lax.fori_loop(0, BLOCKS, reduced, 0)

    def gone(i, carry):
        o = lax.rem(me + i, GROUP)
        value_copy(o, me).wait_send()
        id_copy(o, me).wait_send()
        return carry

    lax.fori_loop(1, GROUP, gone, 0)


def update_kernel(touched_ref, total_ref, table_ref, accum_ref, table_out, accum_out, at_block):
    table_out[...] = table_ref[...]
    accum_out[...] = accum_ref[...]
    at_block[...] = jnp.zeros_like(at_block)
    for j in range(BLOCKS):
        at_block[j : j + 1, :] = accum_ref[pl.ds(touched_ref[j], 1), :]
    old = at_block[...].T
    new = old
    lanes = iota((ROWS, ROWS), 1)
    for j in range(BLOCKS):
        gradient = total_ref[j]
        rows = old[:, j : j + 1] + jnp.sum(gradient * gradient, axis=1, keepdims=True) * (1.0 / D)
        new = jnp.where(lanes == j, rows, new)
        first = pl.multiple_of(touched_ref[j] * ROWS, ROWS)
        table_out[pl.ds(first, ROWS), :] = table_ref[pl.ds(first, ROWS), :] - (
            learning_rate * gradient / (jnp.sqrt(rows) + epsilon)
        )
    at_block[...] = new.T
    for j in range(BLOCKS):
        accum_out[pl.ds(touched_ref[j], 1), :] = at_block[j : j + 1, :]


def on_device(
    pooled_grad, bag_lengths, slot_ids, offsets, touched_blocks, embedding_table, accumulator
):
    vmem = pl.BlockSpec(memory_space=pltpu.VMEM)
    smem = pl.BlockSpec(memory_space=pltpu.SMEM)
    dma = pltpu.SemaphoreType.DMA
    total = pl.pallas_call(
        gather_kernel,
        out_shape=jax.ShapeDtypeStruct((BLOCKS, ROWS, D), F32),
        in_specs=[vmem] * 4,
        out_specs=vmem,
        scratch_shapes=[
            pltpu.VMEM((GROUP, CAP, D), F32),
            pltpu.VMEM((GROUP, CAP, D), F32),
            pltpu.VMEM((GROUP, 1, 128), F32),
            pltpu.VMEM((GROUP, 1, 128), F32),
            pltpu.VMEM((GROUP * CAP, 2 * D), BF16),
            pltpu.VMEM((LOOKUPS, 2 * D), BF16),
            pltpu.VMEM((BLOCKS, ROWS, D), F32),
            pltpu.VMEM((BLOCKS, ROWS, D), F32),
            pltpu.VMEM((BLOCKS, ROWS, D), F32),
            dma((GROUP,)), dma((GROUP,)), dma((GROUP,)), dma((GROUP,)),
            dma((BLOCKS,)), dma((BLOCKS,)), dma((BLOCKS,)),
            dma((BLOCKS, 3)), dma((BLOCKS,)),
        ],
        compiler_params=pltpu.CompilerParams(
            collective_id=0, has_side_effects=True, vmem_limit_bytes=40 << 20
        ),
        name="exchange",
    )(pooled_grad, bag_lengths, slot_ids.reshape(8, 128), offsets.reshape(8, 128))
    rows = embedding_table.shape[0]
    new_table, new_accumulator = pl.pallas_call(
        update_kernel,
        out_shape=(
            jax.ShapeDtypeStruct((rows, D), F32),
            jax.ShapeDtypeStruct((rows // ROWS, ROWS), F32),
        ),
        in_specs=[smem, vmem, vmem, vmem],
        out_specs=(vmem, vmem),
        scratch_shapes=[pltpu.VMEM((ROWS, ROWS), F32)],
        compiler_params=pltpu.CompilerParams(vmem_limit_bytes=40 << 20),
        name="adagrad",
    )(touched_blocks, total, embedding_table, accumulator.reshape(rows // ROWS, ROWS))
    return new_table, new_accumulator.reshape(rows)


def solution(mesh):
    return jax.shard_map(
        on_device,
        mesh=mesh,
        in_specs=(
            P(("replica", "shard"), None),
            P(("replica", "shard"), None),
            P(("replica", "shard")),
            P(("replica", "shard")),
            P("shard"),
            P("shard", None),
            P("shard"),
        ),
        out_specs=(P("shard", None), P("shard")),
        check_vma=False,
    )
```

time: 629 us -> 126 us (0.20)
  the two profiles are of different devices: /device:TPU:2 before, /device:TPU:40 now
where the time goes in v1:
time: 126 us
  Pallas kernels  119 us (94%)
  local copies, waits for them, and re-layouts  5.62 us (4%)
    pallas_call x1, Pallas kernels, on_device(): pl.pallas_call(gather_kernel, out_shape=jax.ShapeDtypeStruct((BLOCKS, ROW...  116 us
    unnamed x14, local copies, waits for them, and re-layouts  5.62 us
    pallas_call x1, Pallas kernels, on_device(): pl.pallas_call(update_kernel, out_shape=(jax.ShapeDtypeStruct((rows, D),...  2.82 us

profile of v1, /device:TPU:40, one launch (start us, length us, event | category | flops | bytes accessed | tf_op | source)
XLA Modules:
  0.0 125.5 jit_solution(13060891534414992814)
XLA Ops:
  0.6 0.0 copy-start.1
  0.6 0.8 copy-done.1
  1.5 0.0 copy-start.3
  1.5 0.7 copy-done.3
  2.2 0.0 copy-start.4
  2.2 0.7 copy-done.4
  2.8 0.0 copy-start.6
  2.8 0.7 copy-done.6
  3.5 116.4 %exchange.1.total_ref = f32[8,128,128]{2,1,0:T(8,128)S(1)} custom-call(f32[128,128]{1,0:T(8,128)S(1)} %copy-done.1, s32[1,128]{1,0:T(1,128)S(1)} %copy-done.6, s32[8,128]{1,0:T(8,128)S(1)} %bitcast.5, s32[8,128]{1,0:T(8,128)S(1)} %bitcast.6), custom_call_target="tpu_custom_call" | custom-call | tf_op jit(solution)/shard_map/exchange/pallas_call | solution.py:337
  119.9 0.0 copy-start
  119.9 1.4 %copy-done = f32[3072,128]{1,0:T(8,128)S(1)} copy-done((f32[3072,128]{1,0:T(8,128)S(1)}, f32[3072,128]{1,0:T(8,128)}, u32[]{:S(2)}) %copy-start) | copy-done | bytes 1572888
  121.3 0.0 copy-start.2
  121.3 0.7 copy-done.2
  122.0 0.0 copy-start.5
  122.0 0.7 copy-done.5
  122.7 2.8 %adagrad.1 = (f32[3072,128]{1,0:T(8,128)}, f32[24,128]{1,0:T(8,128)}) custom-call(s32[8]{0:T(128)S(1)} %copy-done.5, f32[8,128,128]{2,1,0:T(8,128)S(1)} %exchange.1.total_ref, f32[3072,128]{1,0:T(8,128)S(1)} %copy-done, f32[24,128]{1,0:T(8,128)S(1)} %bitcast.4), custom_call_target="tpu_custom_call" | custom-call | tf_op jit(solution)/shard_map/adagrad/pallas_call | solution.py:362
Async XLA Ops:
  0.6 0.8 copy-start.1
  1.5 0.7 copy-start.3
  2.2 0.7 copy-start.4
  2.8 0.7 copy-start.6
  119.9 1.4 %copy-start = (f32[3072,128]{1,0:T(8,128)S(1)}, f32[3072,128]{1,0:T(8,128)}, u32[]{:S(2)}) copy-start(f32[3072,128]{1,0:T(8,128)} %table_ref.1) | copy-start | bytes 4718596
  121.3 0.7 copy-start.2
  122.0 0.7 copy-start.5

commit v2 on v1

v2 whole, which is shorter than its diff:
```python
import jax
import jax.numpy as jnp
from jax import lax
from jax.experimental import pallas as pl
from jax.experimental.pallas import tpu as pltpu
from jax.sharding import PartitionSpec as P

MESH = pl.DeviceIdType.MESH
F32, BF16, I32 = jnp.float32, jnp.bfloat16, jnp.int32

learning_rate = 0.5
epsilon = 1e-08

GROUP = 64
CAP = 32
BLOCKS = 8
ROWS = 128
D = 128
LOOKUPS = 1024
PIECES, PIECE = 16, 64
HOLDERS = 4


def dot(a, b):
    return lax.dot_general(a, b, (((1,), (0,)), ((), ())), preferred_element_type=F32)


def dot_t(a, b):
    return lax.dot_general(a, b, (((1,), (1,)), ((), ())), preferred_element_type=F32)


def iota(shape, dim):
    return lax.broadcasted_iota(I32, shape, dim)


def halves(x):
    high = x.astype(BF16)
    return high, (x - high.astype(F32)).astype(BF16)


def rows_side_by_side(parts):
    return jnp.concatenate(parts, axis=1)


def gather_kernel(
    grad_hbm, len_hbm, slot_hbm, off_hbm, total_ref,
    grad_ref, len_ref, slot_ref, off_ref, sbuf, rbuf, rhl, looked, partial,
    left_in, left_side, right_in, right_side,
    copy_sem, send_sem, recv_sem, red_send,
    left_sem, left_side_sem, right_sem, right_side_sem, out_send, out_sem,
):
    loads = [
        pltpu.make_async_copy(src, dst, copy_sem.at[i])
        for i, (src, dst) in enumerate(
            ((grad_hbm, grad_ref), (len_hbm, len_ref), (slot_hbm, slot_ref), (off_hbm, off_ref))
        )
    ]
    for load in loads:
        load.start()

    replica, shard = lax.axis_index("replica"), lax.axis_index("shard")
    z = lax.div(shard, 32) * 16 + replica
    within = lax.rem(shard, 32)
    parity = lax.rem(z, 2)
    sign = 1 - 2 * parity

    def number(plane, y_at, rest):
        return plane * 32 + lax.rem(y_at - lax.div(rest, 2) + 4, 4) * 8 + rest

    me = number(parity, lax.div(within, 8), lax.rem(within, 8))

    def device(z_at, place):
        return (lax.rem(z_at, 16), lax.div(z_at, 16) * 32 + place)

    def member(o):
        rest = lax.rem(o, 8)
        y_at = lax.rem(lax.div(o, 8) + lax.div(rest, 2), 4)
        return device(z - parity + lax.div(o, 32), y_at * 8 + rest)

    seat = parity * lax.div(31 - z, 2) + (1 - parity) * lax.div(z, 2)

    def along(steps):
        return device(lax.rem(z + sign * steps + 32, 32), within)

    left, right, far_left, far_right = along(-2), along(2), along(-4), along(4)
    twin, inner = along(1), along(-1)

    barrier = pltpu.get_barrier_semaphore()

    def greet(i, carry):
        pl.semaphore_signal(
            barrier, inc=1, device_id=member(lax.rem(me + i, GROUP)), device_id_type=MESH
        )
        return carry

    for other in (left, right, far_left, far_right, inner):
        pl.semaphore_signal(barrier, inc=1, device_id=other, device_id_type=MESH)
    lax.fori_loop(1, GROUP, greet, 0)
    for load in loads:
        load.wait()

    row, col = iota((128, 128), 0), iota((128, 128), 1)
    upto = (row <= col).astype(F32).astype(BF16)
    before = (row < col).astype(F32).astype(BF16)
    lengths = len_ref[...].astype(F32)
    ends = dot(jnp.broadcast_to(lengths, (8, 128)).astype(BF16), upto)[0:1, :]
    starts = ends - lengths
    position = iota((LOOKUPS, 128), 0).astype(F32)
    sample_hot = jnp.where((position >= starts) & (position < ends), 1.0, 0.0).astype(BF16)
    high, low = halves(grad_ref[...])
    looked[...] = dot(sample_hot, jnp.concatenate([high, low], axis=1)).astype(BF16)

    slots = slot_ref[...]
    listed = lax.rem(slots, BLOCKS)
    index = lax.div(slots, BLOCKS)
    owner = number(lax.div(index, 32), lax.rem(lax.div(index, 8), 4), lax.rem(index, 8))
    owner_hot = [
        jnp.where(owner[b : b + 1, :] == iota((GROUP, 128), 0), 1.0, 0.0) for b in range(8)
    ]
    counts = dot(jnp.concatenate(owner_hot, axis=0).astype(BF16), before)
    seen = jnp.zeros((GROUP, 1), F32)
    ranks = []
    for b in range(8):
        earlier = counts[b * GROUP : (b + 1) * GROUP, :] + seen
        ranks.append(jnp.sum(owner_hot[b] * earlier, axis=0, keepdims=True))
        seen = seen + jnp.sum(owner_hot[b], axis=1, keepdims=True)
    rank = rows_side_by_side(ranks)
    owner_row = rows_side_by_side([owner[b : b + 1, :] for b in range(8)])
    place = owner_row * CAP + rank.astype(I32)
    owners = rows_side_by_side([h.astype(BF16) for h in owner_hot])
    lane = rank.astype(I32) + CAP * lax.rem(me, 4)
    at_lane = lane == iota((128, LOOKUPS), 0)
    listed_row = rows_side_by_side([listed[b : b + 1, :] for b in range(8)]).astype(F32)
    offset_row = rows_side_by_side([off_ref[b : b + 1, :] for b in range(8)]).astype(F32)
    ids = 128.0 * dot_t(owners, jnp.where(at_lane, listed_row + 1.0, 0.0).astype(BF16)) + dot_t(
        owners, jnp.where(at_lane, offset_row, 0.0).astype(BF16)
    )
    for o in range(GROUP):
        sbuf[o, CAP : CAP + 1, :] = ids[o : o + 1, :]

    pl.semaphore_wait(barrier, GROUP + 4)

    def value_copy(o, src):
        return pltpu.make_async_remote_copy(
            sbuf.at[o, pl.ds(0, CAP + 1)], rbuf.at[src, pl.ds(0, CAP + 1)], send_sem.at[o], recv_sem.at[src],
            device_id=member(o), device_id_type=MESH,
        )

    my_oct = lax.div(me, 8)

    def send(i, carry):
        oct_at = lax.rem(my_oct + 1 + i, 8)
        hot = jnp.where(place - oct_at * 256 == iota((256, LOOKUPS), 0), 1.0, 0.0).astype(BF16)
        both = dot(hot, looked[...])
        sbuf[pl.ds(oct_at * 8, 8), pl.ds(0, CAP), :] = (both[:, :D] + both[:, D:]).reshape(8, CAP, D)
        for r in range(8):
            o = oct_at * 8 + lax.rem(me + r, 8)

            @pl.when(o != me)
            def _():
                value_copy(o, me).start()

        return carry

    lax.fori_loop(0, 8, send, 0)
    rbuf[me, pl.ds(0, CAP), :] = sbuf[me, pl.ds(0, CAP), :]
    rbuf[me, pl.ds(CAP, 1), :] = sbuf[me, pl.ds(CAP, 1), :]

    def arrive(i, carry):
        src = lax.rem(me + i, GROUP)
        value_copy(src, src).wait_recv()
        return carry

    lax.fori_loop(1, GROUP, arrive, 0)

    id_row = rows_side_by_side(
        [sum(rbuf[4 * g + r, CAP : CAP + 1, :] for r in range(4)) for g in range(16)]
    ).astype(I32)
    high, low = halves(rbuf[:, :CAP, :].reshape(GROUP * CAP, D))
    rhl[:, :D] = high
    rhl[:, D:] = low

    def own_pieces(h):
        hot = jnp.where(
            id_row - (h * 256 + 128) == iota((256, GROUP * CAP), 0), 1.0, 0.0
        ).astype(BF16)
        both = dot(hot, rhl[...])
        partial[pl.ds(h * 4, 4)] = (both[:, :D] + both[:, D:]).reshape(4, PIECE, D)

    def hop(q, into, sem, target):
        return pltpu.make_async_remote_copy(
            partial.at[q], into.at[q], red_send.at[q], sem.at[q],
            device_id=target, device_id_type=MESH,
        )

    def side_step(h, into, sem, target):
        @pl.when(h < HOLDERS)
        def _():
            own_pieces(h)

            def one(k, carry):
                hop(h * 4 + k, into, sem, target).start()
                return carry

            lax.fori_loop(0, 4, one, 0)

    def place_of(steps):
        return lax.rem(seat - 2 + steps + 32, 16)

    def reduce_step(t, carry):
        ahead = 8 - 2 * t
        h_left, h_right = place_of(-ahead), place_of(ahead)
        leads_left, leads_right = h_left < HOLDERS, (h_right < HOLDERS) & (t > 0)

        @pl.when(leads_left & (t == 0))
        def _():
            own_pieces(h_left)

            def one(k, carry):
                hop(h_left * 4 + k, left_in, left_sem, far_left).start()
                return carry

            lax.fori_loop(0, 4, one, 0)

        side_step(place_of(1 - ahead), left_side, left_side_sem, left)
        side_step(place_of(ahead - 1), right_side, right_side_sem, right)

        @pl.when(leads_left & (t > 0))
        def _():
            own_pieces(h_left)

        @pl.when(leads_right)
        def _():
            own_pieces(h_right)

        def one(k, carry):
            @pl.when(leads_left & (t > 0))
            def _():
                q = h_left * 4 + k
                hop(q, left_side, left_side_sem, left).wait_recv()
                hop(q, left_in, left_sem, far_left).wait_recv()
                partial[q] = partial[q] + left_side[q] + left_in[q]
                hop(q, left_in, left_sem, far_left).start()

            @pl.when(leads_right)
            def _():
                q = h_right * 4 + k
                hop(q, right_side, right_side_sem, right).wait_recv()

                @pl.when(t > 1)
                def _():
                    hop(q, right_in, right_sem, far_right).wait_recv()
                    partial[q] = partial[q] + right_in[q]

                partial[q] = partial[q] + right_side[q]
                hop(q, right_in, right_sem, far_right).start()

            return carry

        lax.fori_loop(0, 4, one, 0)
        return carry

    lax.fori_loop(0, 4, reduce_step, 0)

    def out_copy(q, way, target):
        return pltpu.make_async_remote_copy(
            total_ref.at[q], total_ref.at[q], out_send.at[q, way], out_sem.at[q],
            device_id=target, device_id_type=MESH,
        )

    main = seat < 8
    mine = seat - 2
    holds = (seat >= 2) & (seat < 2 + HOLDERS)

    @pl.when(holds)
    def _():
        own_pieces(mine)

        def one(k, carry):
            q = mine * 4 + k
            hop(q, left_side, left_side_sem, left).wait_recv()
            hop(q, right_side, right_side_sem, right).wait_recv()
            hop(q, right_in, right_sem, far_right).wait_recv()
            hop(q, left_in, left_sem, far_left).wait_recv()
            total_ref[q] = (
                partial[q] + left_side[q] + right_side[q] + left_in[q] + right_in[q]
            )
            out_copy(q, 0, left).start()
            out_copy(q, 1, right).start()
            return carry

        lax.fori_loop(0, 4, one, 0)

    @pl.when(main)
    def _():
        def pass_on(s, carry):
            def one(k, carry):
                @pl.when((mine + s >= 0) & (mine + s < HOLDERS))
                def _():
                    q = (mine + s) * 4 + k
                    out_copy(q, 0, left).wait_recv()

                    @pl.when(seat > 0)
                    def _():
                        out_copy(q, 0, left).start()

                    out_copy(q, 2, twin).start()

                @pl.when((mine - s >= 0) & (mine - s < HOLDERS))
                def _():
                    q = (mine - s) * 4 + k
                    out_copy(q, 1, right).wait_recv()

                    @pl.when(seat < 7)
                    def _():
                        out_copy(q, 1, right).start()

                    out_copy(q, 2, inner).start()

                    @pl.when(seat == 7)
                    def _():
                        out_copy(q, 3, twin).start()

                return carry

            return lax.fori_loop(0, 4, one, carry)

        lax.fori_loop(1, 6, pass_on, 0)

        def sent(q, carry):
            h = lax.div(q, 4)

            @pl.when((h >= mine) & (seat > 0))
            def _():
                out_copy(q, 0, left).wait_send()

            @pl.when((h <= mine) & (seat < 7))
            def _():
                out_copy(q, 1, right).wait_send()

            @pl.when(h != mine)
            def _():
                out_copy(q, 2, twin).wait_send()

            @pl.when(seat == 7)
            def _():
                out_copy(q, 3, twin).wait_send()

            return carry

        lax.fori_loop(0, PIECES, sent, 0)

    @pl.when(jnp.logical_not(main))
    def _():
        def land(q, carry):
            out_copy(q, 2, twin).wait_recv()
            return carry

        lax.fori_loop(0, PIECES, land, 0)

    def reduced(q, carry):
        @pl.when(lax.div(q, 4) != mine)
        def _():
            hop(q, left_in, left_sem, left).wait_send()

        return carry

    lax.fori_loop(0, PIECES, reduced, 0)

    def gone(i, carry):
        o = lax.rem(me + i, GROUP)
        value_copy(o, me).wait_send()
        return carry

    lax.fori_loop(1, GROUP, gone, 0)


def update_kernel(
    touched_hbm, total_hbm, table_hbm, accum_hbm, table_out, accum_out,
    total_ref, table_ref, accum_ref, at_block, touched_ref, sem,
):
    load_total = pltpu.make_async_copy(total_hbm, total_ref, sem.at[5])
    load_total.start()
    load_touched = pltpu.make_async_copy(touched_hbm, touched_ref, sem.at[4])
    load_touched.start()
    load_table = pltpu.make_async_copy(table_hbm, table_ref, sem.at[0])
    load_accum = pltpu.make_async_copy(accum_hbm, accum_ref, sem.at[1])
    load_accum.start()
    load_table.start()
    load_total.wait()
    squares = [
        jnp.sum(total_ref[j] * total_ref[j], axis=1, keepdims=True) * (1.0 / D)
        for j in range(BLOCKS)
    ]
    load_touched.wait()
    load_accum.wait()
    at_block[...] = jnp.zeros_like(at_block)
    for j in range(BLOCKS):
        at_block[j : j + 1, :] = accum_ref[pl.ds(touched_ref[j], 1), :]
    old = at_block[...].T
    new = old
    lanes = iota((ROWS, ROWS), 1)
    steps = []
    for j in range(BLOCKS):
        rows = old[:, j : j + 1] + squares[j]
        new = jnp.where(lanes == j, rows, new)
        steps.append(jnp.sqrt(rows) + epsilon)
    at_block[...] = new.T
    for j in range(BLOCKS):
        accum_ref[pl.ds(touched_ref[j], 1), :] = at_block[j : j + 1, :]
    save_accum = pltpu.make_async_copy(accum_ref, accum_out, sem.at[3])
    save_accum.start()
    load_table.wait()
    for j in range(BLOCKS):
        first = pl.multiple_of(touched_ref[j] * ROWS, ROWS)
        table_ref[pl.ds(first, ROWS), :] = table_ref[pl.ds(first, ROWS), :] - (
            learning_rate * total_ref[j] / steps[j]
        )
    save_table = pltpu.make_async_copy(table_ref, table_out, sem.at[2])
    save_table.start()
    save_accum.wait()
    save_table.wait()


def on_device(
    pooled_grad, bag_lengths, slot_ids, offsets, touched_blocks, embedding_table, accumulator
):
    vmem = pl.BlockSpec(memory_space=pltpu.VMEM)
    hbm = pl.BlockSpec(memory_space=pltpu.HBM)
    dma = pltpu.SemaphoreType.DMA
    pieces = pltpu.VMEM((PIECES, PIECE, D), F32)
    total = pl.pallas_call(
        gather_kernel,
        out_shape=jax.ShapeDtypeStruct((PIECES, PIECE, D), F32),
        in_specs=[hbm] * 4,
        out_specs=vmem,
        scratch_shapes=[
            pltpu.VMEM((128, D), F32),
            pltpu.VMEM((1, 128), I32),
            pltpu.VMEM((8, 128), I32),
            pltpu.VMEM((8, 128), I32),
            pltpu.VMEM((GROUP, CAP + 8, D), F32),
            pltpu.VMEM((GROUP, CAP + 8, D), F32),
            pltpu.VMEM((GROUP * CAP, 2 * D), BF16),
            pltpu.VMEM((LOOKUPS, 2 * D), BF16),
            pieces, pieces, pieces, pieces, pieces,
            dma((4,)),
            dma((GROUP,)), dma((GROUP,)),
            dma((PIECES,)), dma((PIECES,)), dma((PIECES,)), dma((PIECES,)), dma((PIECES,)),
            dma((PIECES, 4)), dma((PIECES,)),
        ],
        compiler_params=pltpu.CompilerParams(
            collective_id=0, has_side_effects=True, vmem_limit_bytes=63 << 20
        ),
        name="exchange",
    )(pooled_grad, bag_lengths, slot_ids.reshape(8, 128), offsets.reshape(8, 128))
    rows = embedding_table.shape[0]
    new_table, new_accumulator = pl.pallas_call(
        update_kernel,
        out_shape=(
            jax.ShapeDtypeStruct((rows, D), F32),
            jax.ShapeDtypeStruct((rows // ROWS, ROWS), F32),
        ),
        in_specs=[hbm, hbm, hbm, hbm],
        out_specs=(hbm, hbm),
        scratch_shapes=[
            pltpu.VMEM((BLOCKS, ROWS, D), F32),
            pltpu.VMEM((rows, D), F32),
            pltpu.VMEM((rows // ROWS, ROWS), F32),
            pltpu.VMEM((ROWS, ROWS), F32),
            pltpu.SMEM((BLOCKS,), I32),
            dma((6,)),
        ],
        compiler_params=pltpu.CompilerParams(vmem_limit_bytes=63 << 20),
        name="adagrad",
    )(
        touched_blocks, total.reshape(BLOCKS, ROWS, D), embedding_table,
        accumulator.reshape(rows // ROWS, ROWS),
    )
    return new_table, new_accumulator.reshape(rows)


def solution(mesh):
    return jax.shard_map(
        on_device,
        mesh=mesh,
        in_specs=(
            P(("replica", "shard"), None),
            P(("replica", "shard"), None),
            P(("replica", "shard")),
            P(("replica", "shard")),
            P("shard"),
            P("shard", None),
            P("shard"),
        ),
        out_specs=(P("shard", None), P("shard")),
        check_vma=False,
    )
```

time: 126 us -> 106 us (0.84)
  the two profiles are of different devices: /device:TPU:40 before, /device:TPU:34 now
where the time goes in v2:
time: 106 us; the launch traced here: 105 us
  Pallas kernels  105 us (99%)
    pallas_call x1, Pallas kernels, on_device(): pl.pallas_call(gather_kernel, out_shape=jax.ShapeDtypeStruct((PIECES, PIE...  102 us
    pallas_call x1, Pallas kernels, on_device(): pl.pallas_call(update_kernel, out_shape=(jax.ShapeDtypeStruct((rows, D),...  3.11 us

profile of v2, /device:TPU:34, one launch (start us, length us, event | category | flops | bytes accessed | tf_op | source)
XLA Modules:
  0.0 105.5 jit_solution(16004500818141364885)
XLA Ops:
  0.6 101.7 %exchange.1 = f32[16,64,128]{2,1,0:T(8,128)} custom-call(f32[128,128]{1,0:T(8,128)} %grad_hbm.1, s32[1,128]{1,0:T(1,128)} %len_hbm.1, s32[8,128]{1,0:T(8,128)} %bitcast.7, s32[8,128]{1,0:T(8,128)} %bitcast.8), custom_call_target="tpu_custom_call" | custom-call | tf_op jit(solution)/shard_map/exchange/pallas_call | solution.py:432
  102.4 3.1 %adagrad.1 = (f32[3072,128]{1,0:T(8,128)}, f32[24,128]{1,0:T(8,128)}) custom-call(s32[8]{0:T(128)} %touched_hbm.1, f32[8,128,128]{2,1,0:T(8,128)} %bitcast.5, f32[3072,128]{1,0:T(8,128)} %table_hbm.1, f32[24,128]{1,0:T(8,128)} %bitcast.6), custom_call_target="tpu_custom_call" | custom-call | tf_op jit(solution)/shard_map/adagrad/pallas_call | solution.py:458

commit v3 on v2

--- a/solution.py
+++ b/solution.py
@@ -15,10 +15,13 @@
 CAP = 32
 BLOCKS = 8
 ROWS = 128
+PART = 6
 D = 128
 LOOKUPS = 1024
-PIECES, PIECE = 16, 64
-HOLDERS = 4
+FIRST, HOLDERS = 2, 4
+EACH, PIECE = 4, 64
+HELD = EACH * PIECE
+PIECES = HOLDERS * EACH
 
 
 def dot(a, b):
@@ -59,23 +62,27 @@
         load.start()
 
     replica, shard = lax.axis_index("replica"), lax.axis_index("shard")
-    z = lax.div(shard, 32) * 16 + replica
-    within = lax.rem(shard, 32)
+    high_z, within = lax.div(shard, 32), lax.rem(shard, 32)
+    z = high_z * 16 + replica
     parity = lax.rem(z, 2)
     sign = 1 - 2 * parity
 
+    def device(z_at, place):
+        return (lax.rem(z_at, 16), lax.div(z_at, 16) * 32 + place)
+
     def number(plane, y_at, rest):
         return plane * 32 + lax.rem(y_at - lax.div(rest, 2) + 4, 4) * 8 + rest
 
-    me = number(parity, lax.div(within, 8), lax.rem(within, 8))
-
-    def device(z_at, place):
-        return (lax.rem(z_at, 16), lax.div(z_at, 16) * 32 + place)
-
-    def member(o):
-        rest = lax.rem(o, 8)
-        y_at = lax.rem(lax.div(o, 8) + lax.div(rest, 2), 4)
-        return device(z - parity + lax.div(o, 32), y_at * 8 + rest)
+    my_rest = lax.rem(within, 8)
+    me = number(parity, lax.div(within, 8), my_rest)
+    my_oct = lax.div(me, 8)
+
+    def member(oct_at, rest):
+        y_at = lax.rem(oct_at + lax.div(rest, 2), 4)
+        return (
+            replica - parity + lax.div(oct_at, 4),
+            high_z * 32 + y_at * 8 + rest,
+        )
 
     seat = parity * lax.div(31 - z, 2) + (1 - parity) * lax.div(z, 2)
 
@@ -83,19 +90,28 @@
         return device(lax.rem(z + sign * steps + 32, 32), within)
 
     left, right, far_left, far_right = along(-2), along(2), along(-4), along(4)
-    twin, inner = along(1), along(-1)
+    twin, inner, twin_right, inner_left = along(1), along(-1), along(3), along(-3)
 
     barrier = pltpu.get_barrier_semaphore()
 
     def greet(i, carry):
-        pl.semaphore_signal(
-            barrier, inc=1, device_id=member(lax.rem(me + i, GROUP)), device_id_type=MESH
-        )
+        oct_at = lax.rem(my_oct + i, 8)
+        plane = replica - parity + lax.div(oct_at, 4)
+        for x_at in range(4):
+            place = high_z * 32 + lax.rem(oct_at + x_at, 4) * 8 + x_at * 2
+            for core in range(2):
+
+                @pl.when(oct_at * 8 + x_at * 2 + core != me)
+                def _():
+                    pl.semaphore_signal(
+                        barrier, inc=1, device_id=(plane, place + core), device_id_type=MESH
+                    )
+
         return carry
 
-    for other in (left, right, far_left, far_right, inner):
+    for other in (left, right, far_left, far_right, inner, twin_right, inner_left):
         pl.semaphore_signal(barrier, inc=1, device_id=other, device_id_type=MESH)
-    lax.fori_loop(1, GROUP, greet, 0)
+    lax.fori_loop(0, 8, greet, 0)
     for load in loads:
         load.wait()
 
@@ -138,15 +154,14 @@
     for o in range(GROUP):
         sbuf[o, CAP : CAP + 1, :] = ids[o : o + 1, :]
 
-    pl.semaphore_wait(barrier, GROUP + 4)
-
-    def value_copy(o, src):
+    pl.semaphore_wait(barrier, GROUP + 6)
+
+    def value_copy(o, src, target):
         return pltpu.make_async_remote_copy(
-            sbuf.at[o, pl.ds(0, CAP + 1)], rbuf.at[src, pl.ds(0, CAP + 1)], send_sem.at[o], recv_sem.at[src],
-            device_id=member(o), device_id_type=MESH,
+            sbuf.at[o, pl.ds(0, CAP + 1)], rbuf.at[src, pl.ds(0, CAP + 1)],
+            send_sem.at[o], recv_sem.at[src],
+            device_id=target, device_id_type=MESH,
         )
-
-    my_oct = lax.div(me, 8)
 
     def send(i, carry):
         oct_at = lax.rem(my_oct + 1 + i, 8)
@@ -154,11 +169,12 @@
         both = dot(hot, looked[...])
         sbuf[pl.ds(oct_at * 8, 8), pl.ds(0, CAP), :] = (both[:, :D] + both[:, D:]).reshape(8, CAP, D)
         for r in range(8):
-            o = oct_at * 8 + lax.rem(me + r, 8)
+            rest = lax.rem(my_rest + r, 8)
+            o = oct_at * 8 + rest
 
             @pl.when(o != me)
             def _():
-                value_copy(o, me).start()
+                value_copy(o, me, member(oct_at, rest)).start()
 
         return carry
 
@@ -166,9 +182,18 @@
     rbuf[me, pl.ds(0, CAP), :] = sbuf[me, pl.ds(0, CAP), :]
     rbuf[me, pl.ds(CAP, 1), :] = sbuf[me, pl.ds(CAP, 1), :]
 
+    def split_rows(src):
+        high, low = halves(rbuf[src, pl.ds(0, CAP), :])
+        rows = pl.ds(pl.multiple_of(src * CAP, CAP), CAP)
+        rhl[rows, pl.ds(0, D)] = high
+        rhl[rows, pl.ds(D, D)] = low
+
+    split_rows(me)
+
     def arrive(i, carry):
-        src = lax.rem(me + i, GROUP)
-        value_copy(src, src).wait_recv()
+        src = lax.rem(me + GROUP - i, GROUP)
+        value_copy(src, src, left).wait_recv()
+        split_rows(src)
         return carry
 
     lax.fori_loop(1, GROUP, arrive, 0)
@@ -176,16 +201,13 @@
     id_row = rows_side_by_side(
         [sum(rbuf[4 * g + r, CAP : CAP + 1, :] for r in range(4)) for g in range(16)]
     ).astype(I32)
-    high, low = halves(rbuf[:, :CAP, :].reshape(GROUP * CAP, D))
-    rhl[:, :D] = high
-    rhl[:, D:] = low
 
     def own_pieces(h):
         hot = jnp.where(
-            id_row - (h * 256 + 128) == iota((256, GROUP * CAP), 0), 1.0, 0.0
+            id_row - (h * HELD + ROWS) == iota((HELD, GROUP * CAP), 0), 1.0, 0.0
         ).astype(BF16)
         both = dot(hot, rhl[...])
-        partial[pl.ds(h * 4, 4)] = (both[:, :D] + both[:, D:]).reshape(4, PIECE, D)
+        partial[pl.ds(h * EACH, EACH)] = (both[:, :D] + both[:, D:]).reshape(EACH, PIECE, D)
 
     def hop(q, into, sem, target):
         return pltpu.make_async_remote_copy(
@@ -199,13 +221,13 @@
             own_pieces(h)
 
             def one(k, carry):
-                hop(h * 4 + k, into, sem, target).start()
+                hop(h * EACH + k, into, sem, target).start()
                 return carry
 
-            lax.fori_loop(0, 4, one, 0)
+            lax.fori_loop(0, EACH, one, 0)
 
     def place_of(steps):
-        return lax.rem(seat - 2 + steps + 32, 16)
+        return lax.rem(seat - FIRST + steps + 32, 16)
 
     def reduce_step(t, carry):
         ahead = 8 - 2 * t
@@ -217,10 +239,10 @@
             own_pieces(h_left)
 
             def one(k, carry):
-                hop(h_left * 4 + k, left_in, left_sem, far_left).start()
+                hop(h_left * EACH + k, left_in, left_sem, far_left).start()
                 return carry
 
-            lax.fori_loop(0, 4, one, 0)
+            lax.fori_loop(0, EACH, one, 0)
 
         side_step(place_of(1 - ahead), left_side, left_side_sem, left)
         side_step(place_of(ahead - 1), right_side, right_side_sem, right)
@@ -236,7 +258,7 @@
         def one(k, carry):
             @pl.when(leads_left & (t > 0))
             def _():
-                q = h_left * 4 + k
+                q = h_left * EACH + k
                 hop(q, left_side, left_side_sem, left).wait_recv()
                 hop(q, left_in, left_sem, far_left).wait_recv()
                 partial[q] = partial[q] + left_side[q] + left_in[q]
@@ -244,7 +266,7 @@
 
             @pl.when(leads_right)
             def _():
-                q = h_right * 4 + k
+                q = h_right * EACH + k
                 hop(q, right_side, right_side_sem, right).wait_recv()
 
                 @pl.when(t > 1)
@@ -257,10 +279,16 @@
 
             return carry
 
-        lax.fori_loop(0, 4, one, 0)
+        lax.fori_loop(0, EACH, one, 0)
         return carry
 
-    lax.fori_loop(0, 4, reduce_step, 0)
+    def gone(i, carry):
+        value_copy(lax.rem(me + i, GROUP), me, left).wait_send()
+        return carry
+
+    reduce_step(0, 0)
+    lax.fori_loop(1, GROUP, gone, 0)
+    lax.fori_loop(1, 4, reduce_step, 0)
 
     def out_copy(q, way, target):
         return pltpu.make_async_remote_copy(
@@ -269,15 +297,15 @@
         )
 
     main = seat < 8
-    mine = seat - 2
-    holds = (seat >= 2) & (seat < 2 + HOLDERS)
+    mine = seat - FIRST
+    holds = (mine >= 0) & (mine < HOLDERS)
 
     @pl.when(holds)
     def _():
         own_pieces(mine)
 
         def one(k, carry):
-            q = mine * 4 + k
+            q = mine * EACH + k
             hop(q, left_side, left_side_sem, left).wait_recv()
             hop(q, right_side, right_side_sem, right).wait_recv()
             hop(q, right_in, right_sem, far_right).wait_recv()
@@ -285,66 +313,133 @@
             total_ref[q] = (
                 partial[q] + left_side[q] + right_side[q] + left_in[q] + right_in[q]
             )
-            out_copy(q, 0, left).start()
-            out_copy(q, 1, right).start()
+            out_copy(q, 0, far_left).start()
+            out_copy(q, 1, far_right).start()
             return carry
 
-        lax.fori_loop(0, 4, one, 0)
+        lax.fori_loop(0, EACH, one, 0)
+
+    def reduced(q, carry):
+        @pl.when(lax.div(q, EACH) != mine)
+        def _():
+            hop(q, left_in, left_sem, left).wait_send()
+
+        return carry
+
+    lax.fori_loop(0, PIECES, reduced, 0)
 
     @pl.when(main)
     def _():
-        def pass_on(s, carry):
+        def pass_on(i, carry):
+            away = i + 2 - 2 * lax.rem(i, 2)
+            even = lax.rem(away, 2) == 0
+
             def one(k, carry):
-                @pl.when((mine + s >= 0) & (mine + s < HOLDERS))
+                @pl.when((mine + away >= 0) & (mine + away < HOLDERS))
                 def _():
-                    q = (mine + s) * 4 + k
+                    q = (mine + away) * EACH + k
                     out_copy(q, 0, left).wait_recv()
 
-                    @pl.when(seat > 0)
+                    @pl.when(even & (seat >= 2))
+                    def _():
+                        out_copy(q, 0, far_left).start()
+
+                    @pl.when(even & (seat == 1))
                     def _():
                         out_copy(q, 0, left).start()
 
-                    out_copy(q, 2, twin).start()
-
-                @pl.when((mine - s >= 0) & (mine - s < HOLDERS))
+                    @pl.when(even)
+                    def _():
+                        out_copy(q, 1, right).start()
+
+                    @pl.when((away != 5) & ((away != 3) | (seat == 0)))
+                    def _():
+                        out_copy(q, 2, twin).start()
+
+                    @pl.when(away == 4)
+                    def _():
+                        out_copy(q, 3, twin_right).start()
+
+                    @pl.when((away == 4) & (seat == 1))
+                    def _():
+                        out_copy(q, 4, inner).start()
+
+                @pl.when((mine - away >= 0) & (mine - away < HOLDERS))
                 def _():
-                    q = (mine - s) * 4 + k
+                    q = (mine - away) * EACH + k
                     out_copy(q, 1, right).wait_recv()
 
-                    @pl.when(seat < 7)
-                    def _():
-                        out_copy(q, 1, right).start()
-
-                    out_copy(q, 2, inner).start()
-
-                    @pl.when(seat == 7)
-                    def _():
-                        out_copy(q, 3, twin).start()
+                    @pl.when(even & (seat <= 5))
+                    def _():
+                        out_copy(q, 0, far_right).start()
+
+                    @pl.when(even & (seat == 6))
+                    def _():
+                        out_copy(q, 0, right).start()
+
+                    @pl.when(even)
+                    def _():
+                        out_copy(q, 1, left).start()
+
+                    @pl.when((away != 5) & ((away != 3) | (seat == 7)))
+                    def _():
+                        out_copy(q, 2, inner).start()
+
+                    @pl.when(away == 4)
+                    def _():
+                        out_copy(q, 3, inner_left).start()
+
+                    @pl.when(((away != 5) & (seat == 7)) | ((away == 4) & (seat == 6)))
+                    def _():
+                        out_copy(q, 4, twin).start()
+
+                    @pl.when((away == 4) & (seat == 6))
+                    def _():
+                        out_copy(q, 5, twin_right).start()
 
                 return carry
 
-            return lax.fori_loop(0, 4, one, carry)
-
-        lax.fori_loop(1, 6, pass_on, 0)
+            return lax.fori_loop(0, EACH, one, carry)
+
+        lax.fori_loop(0, 6, pass_on, 0)
 
         def sent(q, carry):
-            h = lax.div(q, 4)
-
-            @pl.when((h >= mine) & (seat > 0))
+            h = lax.div(q, EACH)
+            even = lax.rem(h + FIRST + seat, 2) == 0
+            outer = ((h > mine) & (seat > 0)) | ((h < mine) & (seat < 7)) | (h == mine)
+
+            @pl.when(even & outer)
             def _():
                 out_copy(q, 0, left).wait_send()
 
-            @pl.when((h <= mine) & (seat < 7))
+            @pl.when(even)
             def _():
                 out_copy(q, 1, right).wait_send()
 
-            @pl.when(h != mine)
+            up = h - mine
+            four = (up == 4) | (up == -4)
+            five = (up == 5) | (up == -5)
+            three = ((up == 3) & (seat > 0)) | ((up == -3) & (seat < 7))
+
+            @pl.when((up != 0) & jnp.logical_not(five) & jnp.logical_not(three))
             def _():
                 out_copy(q, 2, twin).wait_send()
 
-            @pl.when(seat == 7)
+            @pl.when(four)
             def _():
                 out_copy(q, 3, twin).wait_send()
+
+            @pl.when(
+                ((up == 4) & (seat == 1))
+                | ((up == -4) & (seat == 6))
+                | ((seat == 7) & jnp.logical_not(five))
+            )
+            def _():
+                out_copy(q, 4, twin).wait_send()
+
+            @pl.when((up == -4) & (seat == 6))
+            def _():
+                out_copy(q, 5, twin).wait_send()
 
             return carry
 
@@ -358,35 +453,31 @@
 
         lax.fori_loop(0, PIECES, land, 0)
 
-    def reduced(q, carry):
-        @pl.when(lax.div(q, 4) != mine)
-        def _():
-            hop(q, left_in, left_sem, left).wait_send()
-
-        return carry
-
-    lax.fori_loop(0, PIECES, reduced, 0)
-
-    def gone(i, carry):
-        o = lax.rem(me + i, GROUP)
-        value_copy(o, me).wait_send()
-        return carry
-
-    lax.fori_loop(1, GROUP, gone, 0)
-
 
 def update_kernel(
     touched_hbm, total_hbm, table_hbm, accum_hbm, table_out, accum_out,
     total_ref, table_ref, accum_ref, at_block, touched_ref, sem,
 ):
-    load_total = pltpu.make_async_copy(total_hbm, total_ref, sem.at[5])
+    load_total = pltpu.make_async_copy(total_hbm, total_ref, sem.at[0])
     load_total.start()
-    load_touched = pltpu.make_async_copy(touched_hbm, touched_ref, sem.at[4])
+    load_touched = pltpu.make_async_copy(touched_hbm, touched_ref, sem.at[2])
     load_touched.start()
-    load_table = pltpu.make_async_copy(table_hbm, table_ref, sem.at[0])
+    def part(ref, c):
+        return ref.at[pl.ds(c * PART * ROWS, PART * ROWS)]
+
+    parts = table_ref.shape[0] // (PART * ROWS)
+    load_table = [
+        pltpu.make_async_copy(part(table_hbm, c), part(table_ref, c), sem.at[5 + c])
+        for c in range(parts)
+    ]
+    save_table = [
+        pltpu.make_async_copy(part(table_ref, c), part(table_out, c), sem.at[5 + parts + c])
+        for c in range(parts)
+    ]
     load_accum = pltpu.make_async_copy(accum_hbm, accum_ref, sem.at[1])
     load_accum.start()
-    load_table.start()
+    for load in load_table:
+        load.start()
     load_total.wait()
     squares = [
         jnp.sum(total_ref[j] * total_ref[j], axis=1, keepdims=True) * (1.0 / D)
@@ -404,22 +495,25 @@
     for j in range(BLOCKS):
         rows = old[:, j : j + 1] + squares[j]
         new = jnp.where(lanes == j, rows, new)
-        steps.append(jnp.sqrt(rows) + epsilon)
+        steps.append(learning_rate / (jnp.sqrt(rows) + epsilon))
     at_block[...] = new.T
     for j in range(BLOCKS):
         accum_ref[pl.ds(touched_ref[j], 1), :] = at_block[j : j + 1, :]
     save_accum = pltpu.make_async_copy(accum_ref, accum_out, sem.at[3])
     save_accum.start()
-    load_table.wait()
-    for j in range(BLOCKS):
-        first = pl.multiple_of(touched_ref[j] * ROWS, ROWS)
-        table_ref[pl.ds(first, ROWS), :] = table_ref[pl.ds(first, ROWS), :] - (
-            learning_rate * total_ref[j] / steps[j]
-        )
-    save_table = pltpu.make_async_copy(table_ref, table_out, sem.at[2])
-    save_table.start()
+    for c in range(parts):
+        load_table[c].wait()
+        for j in range(BLOCKS):
+
+            @pl.when(lax.div(touched_ref[j], PART) == c)
+            def _():
+                rows = pl.ds(pl.multiple_of(touched_ref[j] * ROWS, ROWS), ROWS)
+                table_ref[rows, :] = table_ref[rows, :] - total_ref[j] * steps[j]
+
+        save_table[c].start()
     save_accum.wait()
-    save_table.wait()
+    for save in save_table:
+        save.wait()
 
 
 def on_device(
@@ -447,7 +541,7 @@
             dma((4,)),
             dma((GROUP,)), dma((GROUP,)),
             dma((PIECES,)), dma((PIECES,)), dma((PIECES,)), dma((PIECES,)), dma((PIECES,)),
-            dma((PIECES, 4)), dma((PIECES,)),
+            dma((PIECES, 6)), dma((PIECES,)),
         ],
         compiler_params=pltpu.CompilerParams(
             collective_id=0, has_side_effects=True, vmem_limit_bytes=63 << 20
@@ -469,7 +563,7 @@
             pltpu.VMEM((rows // ROWS, ROWS), F32),
             pltpu.VMEM((ROWS, ROWS), F32),
             pltpu.SMEM((BLOCKS,), I32),
-            dma((6,)),
+            dma((5 + 2 * (rows // (PART * ROWS)),)),
         ],
         compiler_params=pltpu.CompilerParams(vmem_limit_bytes=63 << 20),
         name="adagrad",

time: 106 us -> 99.9 us (0.942)
  Pallas kernels: 105 us -> 99.1 us
    pallas_call x1, Pallas kernels: 102 us -> 95.5 us  [on_device(): pl.pallas_call(gather_kernel, out_shape=jax.ShapeDtypeStruct((PIECES, PIE...]
where the time goes in v3:
time: 99.9 us; the launch traced here: 99.7 us
  Pallas kernels  99.1 us (99%)
    pallas_call x1, Pallas kernels, on_device(): pl.pallas_call(gather_kernel, out_shape=jax.ShapeDtypeStruct((PIECES, PIE...  95.5 us
    pallas_call x1, Pallas kernels, on_device(): pl.pallas_call(update_kernel, out_shape=(jax.ShapeDtypeStruct((rows, D),...  3.54 us

profile of v3, /device:TPU:34, one launch (start us, length us, event | category | flops | bytes accessed | tf_op | source)
XLA Modules:
  0.0 99.7 jit_solution(10448594892673833045)
XLA Ops:
  0.6 95.5 %exchange.1 = f32[16,64,128]{2,1,0:T(8,128)} custom-call(f32[128,128]{1,0:T(8,128)} %grad_hbm.1, s32[1,128]{1,0:T(1,128)} %len_hbm.1, s32[8,128]{1,0:T(8,128)} %bitcast.7, s32[8,128]{1,0:T(8,128)} %bitcast.8), custom_call_target="tpu_custom_call" | custom-call | tf_op jit(solution)/shard_map/exchange/pallas_call | solution.py:526
  96.2 3.5 %adagrad.1 = (f32[3072,128]{1,0:T(8,128)}, f32[24,128]{1,0:T(8,128)}) custom-call(s32[8]{0:T(128)} %touched_hbm.1, f32[8,128,128]{2,1,0:T(8,128)} %bitcast.5, f32[3072,128]{1,0:T(8,128)} %table_hbm.1, f32[24,128]{1,0:T(8,128)} %bitcast.6), custom_call_target="tpu_custom_call" | custom-call | tf_op jit(solution)/shard_map/adagrad/pallas_call | solution.py:552

commit v4 on v3

--- a/solution.py
+++ b/solution.py
@@ -46,11 +46,11 @@
 
 
 def gather_kernel(
-    grad_hbm, len_hbm, slot_hbm, off_hbm, total_ref,
-    grad_ref, len_ref, slot_ref, off_ref, sbuf, rbuf, rhl, looked, partial,
+    grad_hbm, len_hbm, slot_hbm, off_hbm, total_hbm,
+    total_ref, grad_ref, len_ref, slot_ref, off_ref, sbuf, rbuf, rhl, looked, partial,
     left_in, left_side, right_in, right_side,
     copy_sem, send_sem, recv_sem, red_send,
-    left_sem, left_side_sem, right_sem, right_side_sem, out_send, out_sem,
+    left_sem, left_side_sem, right_sem, right_side_sem, out_send, out_sem, save_sem,
 ):
     loads = [
         pltpu.make_async_copy(src, dst, copy_sem.at[i])
@@ -296,6 +296,9 @@
             device_id=target, device_id_type=MESH,
         )
 
+    def save(q):
+        return pltpu.make_async_copy(total_ref.at[q], total_hbm.at[q], save_sem.at[q])
+
     main = seat < 8
     mine = seat - FIRST
     holds = (mine >= 0) & (mine < HOLDERS)
@@ -315,6 +318,7 @@
             )
             out_copy(q, 0, far_left).start()
             out_copy(q, 1, far_right).start()
+            save(q).start()
             return carry
 
         lax.fori_loop(0, EACH, one, 0)
@@ -364,6 +368,8 @@
                     def _():
                         out_copy(q, 4, inner).start()
 
+                    save(q).start()
+
                 @pl.when((mine - away >= 0) & (mine - away < HOLDERS))
                 def _():
                     q = (mine - away) * EACH + k
@@ -396,6 +402,8 @@
                     @pl.when((away == 4) & (seat == 6))
                     def _():
                         out_copy(q, 5, twin_right).start()
+
+                    save(q).start()
 
                 return carry
 
@@ -449,9 +457,16 @@
     def _():
         def land(q, carry):
             out_copy(q, 2, twin).wait_recv()
+            save(q).start()
             return carry
 
         lax.fori_loop(0, PIECES, land, 0)
+
+    def saved(q, carry):
+        save(q).wait()
+        return carry
+
+    lax.fori_loop(0, PIECES, saved, 0)
 
 
 def update_kernel(
@@ -519,7 +534,6 @@
 def on_device(
     pooled_grad, bag_lengths, slot_ids, offsets, touched_blocks, embedding_table, accumulator
 ):
-    vmem = pl.BlockSpec(memory_space=pltpu.VMEM)
     hbm = pl.BlockSpec(memory_space=pltpu.HBM)
     dma = pltpu.SemaphoreType.DMA
     pieces = pltpu.VMEM((PIECES, PIECE, D), F32)
@@ -527,8 +541,9 @@
         gather_kernel,
         out_shape=jax.ShapeDtypeStruct((PIECES, PIECE, D), F32),
         in_specs=[hbm] * 4,
-        out_specs=vmem,
+        out_specs=hbm,
         scratch_shapes=[
+            pieces,
             pltpu.VMEM((128, D), F32),
             pltpu.VMEM((1, 128), I32),
             pltpu.VMEM((8, 128), I32),
@@ -541,7 +556,7 @@
             dma((4,)),
             dma((GROUP,)), dma((GROUP,)),
             dma((PIECES,)), dma((PIECES,)), dma((PIECES,)), dma((PIECES,)), dma((PIECES,)),
-            dma((PIECES, 6)), dma((PIECES,)),
+            dma((PIECES, 6)), dma((PIECES,)), dma((PIECES,)),
         ],
         compiler_params=pltpu.CompilerParams(
             collective_id=0, has_side_effects=True, vmem_limit_bytes=63 << 20

time: 99.9 us -> 99.9 us (level)
  no operation moved by 1% of the time
where the time goes in v4:
time: 99.9 us; the launch traced here: 99.8 us
  Pallas kernels  99.2 us (99%)
    pallas_call x1, Pallas kernels, on_device(): pl.pallas_call(gather_kernel, out_shape=jax.ShapeDtypeStruct((PIECES, PIE...  95.6 us
    pallas_call x1, Pallas kernels, on_device(): pl.pallas_call(update_kernel, out_shape=(jax.ShapeDtypeStruct((rows, D),...  3.58 us

profile of v4, /device:TPU:34, one launch (start us, length us, event | category | flops | bytes accessed | tf_op | source)
XLA Modules:
  0.0 99.8 jit_solution(12091686608996429796)
XLA Ops:
  0.6 95.6 %exchange.1 = f32[16,64,128]{2,1,0:T(8,128)} custom-call(f32[128,128]{1,0:T(8,128)} %grad_hbm.1, s32[1,128]{1,0:T(1,128)} %len_hbm.1, s32[8,128]{1,0:T(8,128)} %bitcast.7, s32[8,128]{1,0:T(8,128)} %bitcast.8), custom_call_target="tpu_custom_call" | custom-call | tf_op jit(solution)/shard_map/exchange/pallas_call | solution.py:540
  96.2 3.6 %adagrad.1 = (f32[3072,128]{1,0:T(8,128)}, f32[24,128]{1,0:T(8,128)}) custom-call(s32[8]{0:T(128)} %touched_hbm.1, f32[8,128,128]{2,1,0:T(8,128)} %bitcast.5, f32[3072,128]{1,0:T(8,128)} %table_hbm.1, f32[24,128]{1,0:T(8,128)} %bitcast.6), custom_call_target="tpu_custom_call" | custom-call | tf_op jit(solution)/shard_map/adagrad/pallas_call | solution.py:567
